TPU v7x, 128 devices: a whole 4x4x4 slice. The times are simulated.
128 devices in a mesh: loader: 8 (over z, core), encoder: 16 (over x, y).
Axes of the slice: x: 4, y: 4, z: 4, core: 2. Of those that a mesh axis runs over, the one named last changes fastest.
Arguments:
- tokens: bfloat16 [98304, 1152], P(('loader', 'encoder')), may hold values from -60 to 60
- lengths: int32 [8, 48], P('loader'), may hold values from 64 to 512, as said below
- norm_gains: float32 [2, 1152], replicated, may hold values from 0.25 to 1.75
- norm_shifts: float32 [2, 1152], replicated, may hold values from -1.5 to 1.5
- qkv_weight: bfloat16 [1152, 3456], replicated, may hold values from -1 to 1
- qkv_bias: float32 [3456], replicated, may hold values from -3 to 3
- out_weight: bfloat16 [1152, 1152], replicated, may hold values from -0.1875 to 0.1875
- out_bias: float32 [1152], replicated, may hold values from -3 to 3
- up_weight: bfloat16 [1152, 4304], P('loader', 'encoder'), may hold values from -0.1875 to 0.1875
- up_bias: float32 [4304], replicated, may hold values from -3 to 3
- down_weight: bfloat16 [4304, 1152], P('encoder', 'loader'), may hold values from -0.09375 to 0.09375
- down_bias: float32 [1152], replicated, may hold values from -3 to 3
Outputs:
- layer_out: bfloat16 [98304, 1152], P(('loader', 'encoder'))
Inputs may be any that keep to these rules, and one draw needn't show every extreme that they name: `lengths`: each row's counts add up to 12288 exactly; in each row one image has 512 patches and one has 64.
All inputs are finite; a program needn't handle non-finite values.
Results may differ from a plain program's by a relative error of at most 0.012.
The roundings to bfloat16 on the way count: a program that leaves them out, or rounds other values in their place, can miss the bound.
Values may be sent and summed in bfloat16 or wider, within the bound.
A program may use at most 128 MiB of HBM per device.

v0:
```python
import jax
import jax.numpy as jnp
from jax import lax
from jax.sharding import PartitionSpec as P

HEADS = 16
MAXLEN = 512


def padded(x, sides, width):
    for axis, dim in sides:
        size, length = (lax.axis_size(axis), x.shape[dim])
        up = [(i, (i + 1) % size) for i in range(size - 1)]
        down = [(j, i) for i, j in up]
        last = lax.slice_in_dim(x, length - width, length, axis=dim)
        leading = lax.slice_in_dim(x, 0, width, axis=dim)
        before = lax.ppermute(last, axis, up)
        after = lax.ppermute(leading, axis, down)
        x = jnp.concatenate([before, x, after], axis=dim)
    return x


def normalize(values, gain, shift):
    center = values - jnp.mean(values, axis=-1, keepdims=True)
    spread = jnp.mean(center * center, axis=-1, keepdims=True)
    return center * lax.rsqrt(spread + 1e-06) * gain + shift


def block_size(count):
    for candidate in (512, 256, 128):
        if count % candidate == 0:
            return candidate
    return count


def segment_ids(positions, image_ends, group_total):
    inside = (positions >= 0) & (positions < group_total)
    found = jnp.sum((image_ends[None, :] <= positions[:, None]).astype(jnp.int32), axis=1)
    return jnp.where(inside, found, jnp.int32(-1))


def attend(queries, keys, values, query_ids, key_ids, margin):
    count = queries.shape[0]
    step_rows = block_size(count)
    window = step_rows + 2 * margin
    scale = queries.shape[2] ** (-0.5)

    def per_block(block_index):
        start = block_index * step_rows
        query_block = lax.dynamic_slice_in_dim(queries, start, step_rows, 0)
        key_block = lax.dynamic_slice_in_dim(keys, start, window, 0)
        value_block = lax.dynamic_slice_in_dim(values, start, window, 0)
        query_seg = lax.dynamic_slice_in_dim(query_ids, start, step_rows, 0)
        key_seg = lax.dynamic_slice_in_dim(key_ids, start, window, 0)
        scores = (
            jnp.einsum("qhd,khd->hqk", query_block, key_block, preferred_element_type=jnp.float32)
            * scale
        )
        same = query_seg[:, None] == key_seg[None, :]
        scores = jnp.where(same[None], scores, -jnp.inf)
        largest = jnp.max(scores, axis=-1, keepdims=True)
        weights = jnp.exp(scores - largest)
        probs = (weights / jnp.sum(weights, axis=-1, keepdims=True)).astype(jnp.bfloat16)
        result = jnp.einsum("hqk,khd->qhd", probs, value_block, preferred_element_type=jnp.float32)
        return result.astype(jnp.bfloat16)

    blocks = lax.map(per_block, jnp.arange(count // step_rows, dtype=jnp.int32))
    return blocks.reshape(count, queries.shape[1], queries.shape[2])


def per_device(
    tokens,
    lengths,
    norm_gains,
    norm_shifts,
    qkv_weight,
    qkv_bias,
    out_weight,
    out_bias,
    up_weight,
    up_bias,
    down_weight,
    down_bias,
):
    row_count = tokens.shape[0]
    model_width = tokens.shape[1]
    head_size = model_width // HEADS
    margin = MAXLEN
    encoder_count = lax.axis_size("encoder")
    group_total = row_count * encoder_count
    image_ends = jnp.cumsum(lengths[0], dtype=jnp.int32)
    wide = tokens.astype(jnp.float32)
    first = normalize(wide, norm_gains[0], norm_shifts[0]).astype(jnp.bfloat16)
    qkv = (jnp.dot(first, qkv_weight, preferred_element_type=jnp.float32) + qkv_bias).astype(
        jnp.bfloat16
    )
    packed = qkv.reshape(row_count, HEADS, 3, head_size)
    base_row = lax.axis_index("encoder") * row_count
    key_pairs = packed[:, :, 1:]
    extended = padded(key_pairs, (("encoder", 0),), margin)
    positions = base_row + jnp.arange(row_count, dtype=jnp.int32)
    key_positions = base_row - margin + jnp.arange(row_count + 2 * margin, dtype=jnp.int32)
    mixed = attend(
        packed[:, :, 0],
        extended[:, :, 0],
        extended[:, :, 1],
        segment_ids(positions, image_ends, group_total),
        segment_ids(key_positions, image_ends, group_total),
        margin,
    )
    mixed = mixed.reshape(row_count, model_width)
    attended = wide + jnp.dot(mixed, out_weight, preferred_element_type=jnp.float32) + out_bias
    second = normalize(attended, norm_gains[1], norm_shifts[1]).astype(jnp.bfloat16)
    up_rows, down_columns = (
        lax.all_gather(up_weight, "loader", axis=0, tiled=True),
        lax.all_gather(down_weight, "loader", axis=1, tiled=True),
    )
    hidden = jax.nn.gelu(
        jnp.dot(
            second,
            lax.all_gather(up_rows, "encoder", axis=1, tiled=True),
            preferred_element_type=jnp.float32,
        )
        + up_bias,
        approximate=True,
    ).astype(jnp.bfloat16)
    feed = jnp.dot(
        hidden,
        lax.all_gather(down_columns, "encoder", axis=0, tiled=True),
        preferred_element_type=jnp.float32,
    )
    return (attended + feed + down_bias).astype(jnp.bfloat16)


def solution(mesh):
    placed = (
        P(("loader", "encoder"), None),
        P("loader", None),
        P(),
        P(),
        P(),
        P(),
        P(),
        P(),
        P("loader", "encoder"),
        P(),
        P("encoder", "loader"),
        P(),
    )
    return jax.shard_map(
        per_device,
        mesh=mesh,
        in_specs=placed,
        out_specs=P(("loader", "encoder"), None),
        check_vma=False,
    )
```

profile of v0, /device:TPU:6, one launch (start us, length us, event | category | flops | bytes accessed | tf_op | source)
XLA Modules:
  0.0 312.9 jit_solution(16499531732370456591)
XLA Ops:
  6.5 15.0 %all_gather.14 = bf16[269,1152]{0,1:T(8,128)(2,1)S(1)} all-gather(bf16[269,144]{0,1:T(8,128)(2,1)} %param.24), channel_id=1, replica_groups=mesh['loader'=8,'encoder'=16] {'loader'}, dimensions={1}, use_global_device_ids=true | all-gather | bytes 697248 | tf_op jit(solution)/shard_map/all_gather | solution.py:116
  21.6 1.1 copy.37
  22.7 0.0 all-gather.7.cloned.1.call-update
  22.7 0.0 all-gather.5.cloned.1.call-start
  22.8 13.8 %all_gather.12 = bf16[1152,269]{1,0:T(8,128)(2,1)S(1)} all-gather(bf16[144,269]{1,0:T(8,128)(2,1)} %param.22), channel_id=1, replica_groups=mesh['loader'=8,'encoder'=16] {'loader'}, dimensions={0}, use_global_device_ids=true | all-gather | bytes 697248 | tf_op jit(solution)/shard_map/all_gather | solution.py:115
  36.5 1.2 copy.36
  37.7 0.0 all-gather.5.cloned.1.call-update
  37.8 0.0 copy-start.2
  37.8 1.5 slice_reduce_fusion
  39.3 1.8 convert_reduce_fusion
  41.1 2.1 fusion.57
  43.2 0.0 copy-done.10
  43.2 0.0 copy-done.2
  43.2 13.0 %add_convert_fusion = bf16[768,3456]{1,0:T(8,128)(2,1)} fusion(bf16[1152,3456]{1,0:T(8,128)(2,1)} %param.18, f32[3456]{0:T(1024)S(1)} %copy-done.10, bf16[768,1152]{1,0:T(8,128)(2,1)S(1)} %copy-done.2, f32[1152]{0:T(1024)S(1)} %get-tuple-element.51, f32[1152]{0:T(1024)S(1)} %get-tuple-element.74, f32[768]{0:T(1024)S(1)} %add_rsqrt_fusion.1, ...), kind=kOutput, calls=%fused_computation.32 | convolution fusion | flops 6125912064 | bytes 15069696 | tf_op jit(solution)/shard_map/dot_general | solution.py:94
  56.1 7.8 %copy.33 = bf16[768,3456]{0,1:T(8,128)(2,1)} copy(bf16[768,3456]{1,0:T(8,128)(2,1)} %add_convert_fusion) | data formatting | bytes 10616832 | tf_op jit(solution)/shard_map/convert_element_type | solution.py:94
  63.9 5.0 %fusion.83 = (bf16[512,16,2,72]{0,3,2,1:T(8,128)(2,1)}, bf16[512,16,2,72]{0,3,2,1:T(8,128)(2,1)}) fusion(bf16[768,16,3,72]{0,3,2,1:T(8,128)(2,1)} %bitcast.33), kind=kLoop, calls=%fused_computation.79 | loop fusion | bytes 9437184 | tf_op jit(solution)/shard_map/slice | solution.py:15
  68.9 5.3 %collective-permute-start.1 = (bf16[512,16,2,72]{0,3,2,1:T(8,128)(2,1)}, bf16[512,16,2,72]{0,3,2,1:T(8,128)(2,1)}, u32[]{:S(2)}, u32[]{:S(2)}) collective-permute-start(bf16[512,16,2,72]{0,3,2,1:T(8,128)(2,1)} %get-tuple-element.71), channel_id=1, source_target_pairs={{1,0},{2,1},{3,2},{4,3},{5,4},{6,5},{7,6},{8,7},{9,8},{10,9},{11,1... | collective-permute-start | bytes 7077896 | tf_op jit(solution)/shard_map/ppermute | solution.py:18
  74.2 2.4 collective-permute-start
  76.7 0.0 copy-start.8
  76.7 4.1 %slice.43 = bf16[768,16,2,72]{0,3,2,1:T(8,128)(2,1)} slice(bf16[768,16,3,72]{0,3,2,1:T(8,128)(2,1)} %bitcast.34), slice={[0:768], [0:16], [1:3], [0:72]} | slice | bytes 7077888 | tf_op jit(solution)/shard_map/slice | solution.py:99
  80.8 0.1 copy.34
  80.9 0.1 reduce-window.8
  81.0 0.1 reduce.2
  81.1 0.1 convert_reduce_fusion.2
  81.2 0.1 convert_reduce_fusion.1
  81.4 3.1 slice_bitcast_fusion.2
  84.4 72.9 %collective-permute-done.1 = bf16[512,16,2,72]{0,3,2,1:T(8,128)(2,1)} collective-permute-done((bf16[512,16,2,72]{0,3,2,1:T(8,128)(2,1)}, bf16[512,16,2,72]{0,3,2,1:T(8,128)(2,1)}, u32[]{:S(2)}, u32[]{:S(2)}) %collective-permute-start.1) | collective-permute-done | bytes 2359328 | tf_op jit(solution)/shard_map/ppermute | solution.py:18
  157.3 2.2 collective-permute-done
  159.6 3.2 %pad_maximum_fusion = bf16[1792,16,2,72]{0,3,2,1:T(8,128)(2,1)S(1)} fusion(bf16[512,16,2,72]{0,3,2,1:T(8,128)(2,1)} %collective-permute-done.1, bf16[768,16,2,72]{0,3,2,1:T(8,128)(2,1)S(1)} %copy-done.1, bf16[512,16,2,72]{0,3,2,1:T(8,128)(2,1)} %collective-permute-done), kind=kLoop, calls=%fused_computation.33 | loop fusion | flops 24772608 | bytes 16515072 | tf_op jit(solution)/shard_map/concatenate | solution.py:19
  162.8 3.6 %slice_bitcast_fusion = (bf16[1792,16,72]{0,2,1:T(8,128)(2,1)}, bf16[1792,16,72]{0,2,1:T(8,128)(2,1)}) fusion(bf16[1792,16,2,72]{0,3,2,1:T(8,128)(2,1)S(1)} %pad_maximum_fusion), kind=kLoop, calls=%fused_computation.42 | loop fusion | bytes 16515072 | tf_op jit(solution)/shard_map/squeeze | solution.py:105
  166.4 63.6 %while.10 = (s32[]{:T(128)}, bf16[3,256,16,72]{1,3,2,0:T(8,128)(2,1)}, s32[3]{0:T(128)S(1)}, bf16[1792,16,72]{0,2,1:T(8,128)(2,1)}, s32[768]{0:T(1024)S(1)}, /*i...) while((s32[]{:T(128)}, ...), condition=%wide.region_8.9_spmd, body=%wide.region_5.8_spmd.sunk | while | flops 2312739328 | bytes 11653352 | solution.py:67
  166.4 0.7 dynamic_slice.65
  167.8 0.1 dynamic_slice.66
  167.9 0.1 dynamic_slice.67
  167.9 0.3 broadcast_compare_fusion.2
  168.2 8.7 %exponential_reduce_fusion.2 = f32[16,256]{1,0:T(8,128)S(1)} fusion(pred[256,1280]{1,0:T(8,128)(4,1)S(1)} %broadcast_compare_fusion.2, bf16[1792,16,72]{0,2,1:T(8,128)(2,1)} %get-tuple-element.158, s32[]{:T(128)S(6)} %select_n.42, bf16[768,16,72]{0,2,1:T(8,128)(2,1)} %get-tuple-element.157, s32[]{:T(128)S(6)} %select_n.43), kind=kOutput, calls=%fused_computation.4.clone.1 | convolution fusion | flops 775947520 | bytes 3883016 | tf_op jit(solution)/shard_map/while/body/eval_jaxpr/sub | solution.py:62
  176.9 10.6 %fusion.101 = bf16[3,256,16,72]{1,3,2,0:T(8,128)(2,1)} fusion(bf16[3,256,16,72]{1,3,2,0:T(8,128)(2,1)} %get-tuple-element.139, s32[]{:T(128)S(6)} %copy.42, f32[16,256]{1,0:T(8,128)S(1)} %exponential_reduce_fusion.2, bf16[1792,16,72]{0,2,1:T(8,128)(2,1)} %get-tuple-element.154, s32[]{:T(128)S(6)} %select_n.42, ...), kind=kOutput, calls=%fused_computation.10.clone.1 | convolution fusion | flops 1536464128 | bytes 7424000 | tf_op jit(solution)/shard_map/while/body/eval_jaxpr/hqk,khd->qhd/dot_general | solution.py:64
  187.6 0.6 dynamic_slice.65
  188.9 0.1 dynamic_slice.66
  189.0 0.1 dynamic_slice.67
  189.1 0.3 broadcast_compare_fusion.2
  189.3 8.8 %exponential_reduce_fusion.2 = f32[16,256]{1,0:T(8,128)S(1)} fusion(pred[256,1280]{1,0:T(8,128)(4,1)S(1)} %broadcast_compare_fusion.2, bf16[1792,16,72]{0,2,1:T(8,128)(2,1)} %get-tuple-element.158, s32[]{:T(128)S(6)} %select_n.42, bf16[768,16,72]{0,2,1:T(8,128)(2,1)} %get-tuple-element.157, s32[]{:T(128)S(6)} %select_n.43), kind=kOutput, calls=%fused_computation.4.clone.1 | convolution fusion | flops 775947520 | bytes 3883016 | tf_op jit(solution)/shard_map/while/body/eval_jaxpr/sub | solution.py:62
  198.1 10.7 %fusion.101 = bf16[3,256,16,72]{1,3,2,0:T(8,128)(2,1)} fusion(bf16[3,256,16,72]{1,3,2,0:T(8,128)(2,1)} %get-tuple-element.139, s32[]{:T(128)S(6)} %copy.42, f32[16,256]{1,0:T(8,128)S(1)} %exponential_reduce_fusion.2, bf16[1792,16,72]{0,2,1:T(8,128)(2,1)} %get-tuple-element.154, s32[]{:T(128)S(6)} %select_n.42, ...), kind=kOutput, calls=%fused_computation.10.clone.1 | convolution fusion | flops 1536464128 | bytes 7424000 | tf_op jit(solution)/shard_map/while/body/eval_jaxpr/hqk,khd->qhd/dot_general | solution.py:64
  208.8 0.6 dynamic_slice.65
  210.1 0.1 dynamic_slice.66
  210.2 0.1 dynamic_slice.67
  210.3 0.3 broadcast_compare_fusion.2
  210.5 8.7 %exponential_reduce_fusion.2 = f32[16,256]{1,0:T(8,128)S(1)} fusion(pred[256,1280]{1,0:T(8,128)(4,1)S(1)} %broadcast_compare_fusion.2, bf16[1792,16,72]{0,2,1:T(8,128)(2,1)} %get-tuple-element.158, s32[]{:T(128)S(6)} %select_n.42, bf16[768,16,72]{0,2,1:T(8,128)(2,1)} %get-tuple-element.157, s32[]{:T(128)S(6)} %select_n.43), kind=kOutput, calls=%fused_computation.4.clone.1 | convolution fusion | flops 775947520 | bytes 3883016 | tf_op jit(solution)/shard_map/while/body/eval_jaxpr/sub | solution.py:62
  219.2 10.7 %fusion.101 = bf16[3,256,16,72]{1,3,2,0:T(8,128)(2,1)} fusion(bf16[3,256,16,72]{1,3,2,0:T(8,128)(2,1)} %get-tuple-element.139, s32[]{:T(128)S(6)} %copy.42, f32[16,256]{1,0:T(8,128)S(1)} %exponential_reduce_fusion.2, bf16[1792,16,72]{0,2,1:T(8,128)(2,1)} %get-tuple-element.154, s32[]{:T(128)S(6)} %select_n.42, ...), kind=kOutput, calls=%fused_computation.10.clone.1 | convolution fusion | flops 1536464128 | bytes 7424000 | tf_op jit(solution)/shard_map/while/body/eval_jaxpr/hqk,khd->qhd/dot_general | solution.py:64
  230.0 0.0 copy-start.3
  230.1 0.0 copy-start.11
  230.1 3.1 copy.35
  233.2 0.5 copy.38
  233.7 0.0 copy-done
  233.7 0.0 copy-done.3
  233.7 0.0 copy-done.11
  233.7 3.1 %fusion.84 = (f32[768]{0:T(1024)S(1)}, f32[768,1152]{1,0:T(8,128)S(1)}) fusion(f32[1152]{0:T(1024)S(1)} %copy-done.11, bf16[768,1152]{0,1:T(8,128)(2,1)S(1)} %bitcast.39, bf16[1152,1152]{1,0:T(8,128)(2,1)S(1)} %copy-done, bf16[768,1152]{1,0:T(8,128)(2,1)S(1)} %copy-done.3), kind=kOutput, calls=%fused_computation.80 | convolution fusion | flops 2041969920 | bytes 9739776 | tf_op jit(solution)/shard_map/dot_general | solution.py:112
  236.8 1.7 copy-done.4
  238.6 0.5 multiply_reduce_fusion
  239.1 0.0 all-gather.7.cloned.1.call-done
  239.1 12.2 %reshape.100 = bf16[4304,1152]{1,0:T(8,128)(2,1)} reshape(bf16[16,269,1152]{2,1,0:T(8,128)(2,1)} %all-gather.7.cloned.1.call-done) | data formatting | bytes 19832832
  251.3 0.0 all-gather.5.cloned.1.call-done
  251.3 12.4 %reshape.98 = bf16[4304,1152]{1,0:T(8,128)(2,1)} reshape(bf16[16,269,1152]{2,1,0:T(8,128)(2,1)} %all-gather.5.cloned.1.call-done) | data formatting | bytes 19832832
  263.8 42.0 %fusion.61 = bf16[768,1152]{1,0:T(8,128)(2,1)} fusion(f32[768,1152]{1,0:T(8,128)} %copy-done.4, bf16[4304,1152]{1,0:T(8,128)(2,1)} %reshape.100, bf16[4304,1152]{1,0:T(8,128)(2,1)} %reshape.98, f32[4304]{0:T(1024)S(1)} %copy-done.9, f32[1152]{0:T(1024)S(1)} %copy-done.12, f32[1152]{0:T(1024)S(1)} %copy-done.6, f32[1152]{0:T(1024)S(1)} %copy-done.7, ...), kind=kOutput, calls=%fused_computation.51 | convolution fusion | flops 15271747584 | bytes 25178432 | tf_op jit(solution)/shard_map/dot_general | solution.py:127
  (27 shorter events, 0.1 us)
Async XLA Ops:
  6.5 227.1 %copy-start = (bf16[1152,1152]{1,0:T(8,128)(2,1)S(1)}, bf16[1152,1152]{1,0:T(8,128)(2,1)}, u32[]{:S(2)}) copy-start(bf16[1152,1152]{1,0:T(8,128)(2,1)} %param.20) | copy-start | bytes 7962628
  6.5 31.2 %copy-start.5 = (f32[2,1152]{1,0:T(2,128)S(1)}, f32[2,1152]{1,0:T(2,128)}, u32[]{:S(2)}) copy-start(f32[2,1152]{1,0:T(2,128)} %param.17) | copy-start | bytes 27652
  6.5 232.6 %all-gather.7.cloned.1.call-start = ((), (), s32[]{:S(2)}) async-start(), calls=%async_computation.1 | async-start | bytes 10653696 | tf_op jit(solution)/shard_map/all_gather | solution.py:129
  22.7 228.6 %all-gather.5.cloned.1.call-start = ((), (), s32[]{:S(2)}) async-start(), calls=%async_computation | async-start | bytes 10653696 | tf_op jit(solution)/shard_map/all_gather | solution.py:121
  37.7 5.4 %copy-start.10 = (f32[3456]{0:T(1024)S(1)}, f32[3456]{0:T(1024)}, u32[]{:S(2)}) copy-start(f32[3456]{0:T(1024)} %param.19) | copy-start | bytes 41476
  37.8 5.4 %copy-start.2 = (bf16[768,1152]{1,0:T(8,128)(2,1)S(1)}, bf16[768,1152]{1,0:T(8,128)(2,1)}, u32[]{:S(2)}) copy-start(bf16[768,1152]{1,0:T(8,128)(2,1)} %param.14) | copy-start | bytes 5308420
  68.9 88.4 %collective-permute-start.1 = (bf16[512,16,2,72]{0,3,2,1:T(8,128)(2,1)}, bf16[512,16,2,72]{0,3,2,1:T(8,128)(2,1)}, u32[]{:S(2)}, u32[]{:S(2)}) collective-permute-start(bf16[512,16,2,72]{0,3,2,1:T(8,128)(2,1)} %get-tuple-element.71), channel_id=1, source_target_pairs={{1,0},{2,1},{3,2},{4,3},{5,4},{6,5},{7,6},{8,7},{9,8},{10,9},{11,1... | collective-permute-start | bytes 7077896 | tf_op jit(solution)/shard_map/ppermute | solution.py:18
  74.2 85.3 %collective-permute-start = (bf16[512,16,2,72]{0,3,2,1:T(8,128)(2,1)}, bf16[512,16,2,72]{0,3,2,1:T(8,128)(2,1)}, u32[]{:S(2)}, u32[]{:S(2)}) collective-permute-start(bf16[512,16,2,72]{0,3,2,1:T(8,128)(2,1)} %get-tuple-element.70), channel_id=1, source_target_pairs={{0,1},{1,2},{2,3},{3,4},{4,5},{5,6},{6,7},{7,8},{8,9},{9,10},{10,1... | collective-permute-start | bytes 7077896 | tf_op jit(solution)/shard_map/ppermute | solution.py:17
  76.7 4.1 %copy-start.8 = (s32[1,48]{1,0:T(1,128)S(1)}, s32[1,48]{1,0:T(1,128)}, u32[]{:S(2)}) copy-start(s32[1,48]{1,0:T(1,128)} %param.15) | copy-start | bytes 580
  81.1 78.5 %copy-start.1 = (bf16[768,16,2,72]{0,3,2,1:T(8,128)(2,1)S(1)}, bf16[768,16,2,72]{0,3,2,1:T(8,128)(2,1)}, u32[]{:S(2)}) copy-start(bf16[768,16,2,72]{0,3,2,1:T(8,128)(2,1)} %slice.43) | copy-start | bytes 10616836
  230.0 3.6 %copy-start.3 = (bf16[768,1152]{1,0:T(8,128)(2,1)S(1)}, bf16[768,1152]{1,0:T(8,128)(2,1)}, u32[]{:S(2)}) copy-start(bf16[768,1152]{1,0:T(8,128)(2,1)} %param.14) | copy-start | bytes 5308420
  230.1 3.6 %copy-start.11 = (f32[1152]{0:T(1024)S(1)}, f32[1152]{0:T(1024)}, u32[]{:S(2)}) copy-start(f32[1152]{0:T(1024)} %param.21) | copy-start | bytes 13828
  236.8 1.8 copy-start.4
  251.3 12.5 %copy-start.6 = (f32[1152]{0:T(1024)S(1)}, f32[1152]{0:T(1024)}, u32[]{:S(2)}) copy-start(f32[1152]{0:T(1024)} %get-tuple-element.50) | copy-start | bytes 13828
  251.3 12.5 %copy-start.7 = (f32[1152]{0:T(1024)S(1)}, f32[1152]{0:T(1024)}, u32[]{:S(2)}) copy-start(f32[1152]{0:T(1024)} %get-tuple-element.75) | copy-start | bytes 13828
  251.3 12.5 %copy-start.9 = (f32[4304]{0:T(1024)S(1)}, f32[4304]{0:T(1024)}, u32[]{:S(2)}) copy-start(f32[4304]{0:T(1024)} %param.23) | copy-start | bytes 51652
  251.3 12.5 %copy-start.12 = (f32[1152]{0:T(1024)S(1)}, f32[1152]{0:T(1024)}, u32[]{:S(2)}) copy-start(f32[1152]{0:T(1024)} %param.25) | copy-start | bytes 13828
Sparse Core Ops, SparseCore 0:
  22.8 104.8 all-gather.6
  129.9 85.4 all-gather.4
where the time goes:
time: 318 us; the launch traced here: 313 us
  matrix products  116 us (36%)
  waiting for transfers between devices  75.2 us (24%)
  local copies, waits for them, and re-layouts  59.8 us (19%)
  blocking collectives  28.8 us (9%)
  between operations  13.9 us (4%)
  other arithmetic  8.81 us (3%)
  starting transfers between devices  7.81 us (2%)
    ppermute x1, waiting for transfers between devices, padded(): after = lax.ppermute(leading, axis, down)  72.9 us
    dot_general x1, matrix products, per_device(): jnp.dot(hidden, lax.all_gather(down_columns, 'encoder', axis=0, tiled=Tru...  42 us
    dot_general x3, matrix products, per_block(): jnp.einsum('hqk,khd->qhd', probs, value_block, preferred_element_type=jnp...  32 us
    unnamed x31, local copies, waits for them, and re-layouts  29.2 us
    sub x3, matrix products, per_block(): weights = jnp.exp(scores - largest)  26.2 us
    all_gather x1, blocking collectives, per_device(): lax.all_gather(down_weight, 'loader', axis=1, tiled=True)  15 us
    all_gather x1, blocking collectives, per_device(): lax.all_gather(up_weight, 'loader', axis=0, tiled=True)  13.8 us
    dot_general x1, matrix products, per_device(): jnp.dot(first, qkv_weight, preferred_element_type=jnp.float32) + qkv_bias  13 us
  transfers between devices with their start and end apart: 4, of which 2 were waited for; matrix products, arithmetic and copies ran while one was open for 41% of the time, Pallas kernels for 0%

commit v1 on v0

v1 whole, which is shorter than its diff:
```python
import functools

import jax
import jax.numpy as jnp
import numpy as np
from jax import lax
from jax.experimental import pallas as pl
from jax.experimental.pallas import tpu as pltpu
from jax.sharding import PartitionSpec as P

HEADS = 16
HEAD = 72
D = 1152
REACH = 512
ROWS = 768
EXT = ROWS + 2 * REACH
IMAGES = 48
TILE = 256
WINDOW = TILE + 2 * REACH
PARTS = (("xyz", 64, 96), ("yzx", 0, 32), ("xzy", 32, 32))
BLOCK = 160
MAIN = 144
FFB = 256
REM = 13
BIG = -1e30
SCALE = float(HEAD**-0.5 * np.log2(np.e))
NT = (((1,), (1,)), ((), ()))
MESH = pl.DeviceIdType.MESH
F32, BF16 = jnp.float32, jnp.bfloat16


def normalize(values, gain, shift):
    center = values - jnp.mean(values, axis=-1, keepdims=True)
    spread = jnp.mean(center * center, axis=-1, keepdims=True)
    return center * lax.rsqrt(spread + 1e-06) * gain + shift


def gelu(x):
    return 0.5 * x * (1.0 + jnp.tanh(0.7978845608028654 * (x + 0.044715 * (x * x * x))))


def layer_kernel(
    tok, lens, gains, shifts, qkvw_hbm, qkvb, outw_hbm, outb, block, upb, upb_rem, downb,
    out, w,
    halo, qkvw, outw, q_s, k_s, v_s, qx, kx, first, wide, sbuf, mbuf, mixed, acc, hid, hid_r, stage, rest, ru, rd,
    local_sem, stage_sem, halo_send, halo_recv, send, recv, sib_send, sib_recv,
):
    ld, en = lax.axis_index("loader"), lax.axis_index("encoder")
    z, core = ld // 2, ld % 2
    x, y = en // 4, en % 4
    pos = {"x": x, "y": y, "z": z}
    sibling = (z * 2 + 1 - core, en)
    right, left = (ld, (en + 1) % 16), (ld, (en + 15) % 16)

    def device(d, step):
        p = (pos[d] + step) % 4
        if d == "x":
            return (ld, p * 4 + y)
        if d == "y":
            return (ld, x * 4 + p)
        return (p * 2 + core, en)

    qkvw_copy = pltpu.make_async_copy(qkvw_hbm, qkvw, local_sem.at[0])
    outw_copy = pltpu.make_async_copy(outw_hbm, outw, local_sem.at[1])
    own_copy = pltpu.make_async_copy(block, w.at[x, y, :, z, core], local_sem.at[2])
    own_copy.start()
    qkvw_copy.start()
    outw_copy.start()

    barrier = pltpu.get_barrier_semaphore()
    peers = [device(d, s) for d in "xyz" for s in (1, 2, 3)] + [sibling, right, left]
    for peer in peers:
        pl.semaphore_signal(barrier, inc=1, device_id=peer, device_id_type=MESH)
    pl.semaphore_wait(barrier, len(peers))
    own_copy.wait()

    copies = []

    def remote(src, dst, ssem, rsem, to):
        copy = pltpu.make_async_remote_copy(
            src_ref=src, dst_ref=dst, send_sem=ssem, recv_sem=rsem, device_id=to, device_id_type=MESH
        )
        copy.start()
        copies.append(copy)
        return copy

    def region(u, i, phase, at, half):
        order, row, count = PARTS[i]
        index = dict(pos)
        for d in order[:phase]:
            index[d] = pl.ds(0, 4)
        if half is not None:
            index[order[0]] = pl.ds(2 * half, 2)
        index[order[phase]] = at
        return w.at[index["x"], index["y"], u, index["z"], core, pl.ds(row, count)]

    pending = {}

    def move(u, i, phase, at, half, slot, step):
        part = region(u, i, phase, at, half)
        pending[u, i, slot] = remote(
            part, part, send.at[u, i, slot], recv.at[u, i, slot], device(PARTS[i][0][phase], step)
        )

    def to_sibling(u, i, at, half, slot):
        part = region(u, i, 2, at, half)
        pending[u, i, "s", slot] = remote(part, part, sib_send.at[u, i, slot], sib_recv.at[u, i, slot], sibling)

    def phase1(u):
        for i, (order, _, _) in enumerate(PARTS):
            for slot, step in enumerate((1, 3, 2)):
                move(u, i, 0, pos[order[0]], None, slot, step)

    def ring_start(u, phase):
        slot = 3 if phase == 1 else 7
        for i, (order, _, _) in enumerate(PARTS):
            for a in range(3 if phase == 1 else 0):
                pending[u, i, a].wait_recv()
            for s, step in enumerate((1, 3)):
                move(u, i, phase, pos[order[phase]], None, slot + s, step)
            if phase == 2:
                to_sibling(u, i, pos[order[2]], None, 0)

    def ring_forward(u, phase):
        slot = 3 if phase == 1 else 7
        for i, (order, _, _) in enumerate(PARTS):
            for s, step in enumerate((1, 3)):
                pending[u, i, slot + s].wait_recv()
                at = (pos[order[phase]] + 4 - step) % 4
                move(u, i, phase, at, s, slot + 2 + s, step)
                if phase == 2:
                    to_sibling(u, i, at, None, 1 + s)

    def ring_finish(u, phase):
        slot = 3 if phase == 1 else 7
        for i, (order, _, _) in enumerate(PARTS):
            for s in range(2):
                pending[u, i, slot + 2 + s].wait_recv()
                if phase == 2:
                    to_sibling(u, i, (pos[order[2]] + 2) % 4, s, 3 + s)

    def sibling_finish(u):
        for i in range(len(PARTS)):
            for slot in range(5):
                pending[u, i, "s", slot].wait_recv()

    phase1(0)
    halo_copies = {}
    for slot, (row, to) in ((1, (512, right)), (2, (0, left)), (0, (256, right)), (3, (256, left))):
        halo_copies[slot] = remote(
            tok.at[pl.ds(row, 256)], halo.at[slot], halo_send.at[slot], halo_recv.at[slot], to
        )
    phase1(1)

    lengths = lens[...]
    sub = lax.broadcasted_iota(jnp.int32, (IMAGES, IMAGES), 0)
    lan = lax.broadcasted_iota(jnp.int32, (IMAGES, IMAGES), 1)
    ends_column = jnp.sum(jnp.where(lan <= sub, lengths, 0), axis=1, keepdims=True)
    ends = jnp.sum(jnp.where(lan == sub, ends_column, 0), axis=0, keepdims=True)
    base = en * ROWS

    def image_lane(count, offset):
        at = lax.broadcasted_iota(jnp.int32, (count, IMAGES), 0) + (base + offset)
        found = jnp.sum((ends <= at).astype(jnp.int32), axis=1, keepdims=True) + 1
        column = lax.broadcasted_iota(jnp.int32, (count, 1), 0) + (base + offset)
        found = jnp.where(column < 0, 0, found)
        return found + HEAD == lax.broadcasted_iota(jnp.int32, (count, 128), 1)

    def lanes(count):
        return lax.broadcasted_iota(jnp.int32, (count, 128), 1)

    for r in range(0, ROWS, 256):
        qx[r : r + 256] = jnp.where(image_lane(256, r), 0.0, 1.0).astype(BF16)
    for r in range(0, EXT, 256):
        kx[r : r + 256] = jnp.where(image_lane(256, r - REACH), BIG, 0.0).astype(BF16)

    def project(rows_value, row, own):
        first[...] = normalize(rows_value.astype(F32), gains[0:1], shifts[0:1]).astype(BF16)
        for n in range(3):
            cut = slice(n * D, (n + 1) * D)
            product = jnp.dot(first[...], qkvw[:, cut], preferred_element_type=F32) + qkvb[:, cut]
            wide[:, cut] = product.astype(BF16)
        inside = lanes(256) < HEAD
        ones = jnp.where(lanes(256) == HEAD, 1.0, 0.0).astype(BF16)
        for h in range(HEADS):
            for c in range(0 if own else 1, 3):
                lo = h * 3 * HEAD + c * HEAD
                start = lo // 128 * 128
                shift = lo - start
                if shift == 0:
                    piece = wide[:, start : start + 128]
                elif shift + HEAD <= 128:
                    piece = pltpu.roll(wide[:, start : start + 128], 128 - shift, 1)
                else:
                    piece = pltpu.roll(wide[:, start : start + 256], 256 - shift, 1)[:, :128]
                if c == 0:
                    q_s[h, pl.ds(row, 256), :] = jnp.where(inside, piece, qx[pl.ds(row, 256), :])
                elif c == 1:
                    at = row + REACH if own else row
                    k_s[h, pl.ds(at, 256), :] = jnp.where(inside, piece, kx[pl.ds(at, 256), :])
                else:
                    at = row + REACH if own else row
                    v_s[h, pl.ds(at, 256), :] = jnp.where(inside, piece, ones)

    chunk = TILE

    def attention(tile):
        row = tile * TILE

        def scores(h, slot):
            most = None
            for c in range(0, WINDOW, chunk):
                s = lax.dot_general(
                    q_s[h, row : row + TILE, :], k_s[h, row + c : row + c + chunk, :], NT, preferred_element_type=F32
                )
                sbuf[slot, :, c : c + chunk] = s
                for j in range(0, chunk, 128):
                    most = s[:, j : j + 128] if most is None else jnp.maximum(most, s[:, j : j + 128])
            mbuf[slot] = most

        def step(h, now, later):
            peak = jnp.max(mbuf[now], axis=1, keepdims=True) * SCALE
            following = jnp.minimum(h + 1, HEADS - 1)
            total = most = None
            for c in range(0, WINDOW, chunk):
                s = lax.dot_general(
                    q_s[following, row : row + TILE, :],
                    k_s[following, row + c : row + c + chunk, :],
                    NT,
                    preferred_element_type=F32,
                )
                sbuf[later, :, c : c + chunk] = s
                for j in range(0, chunk, 128):
                    most = s[:, j : j + 128] if most is None else jnp.maximum(most, s[:, j : j + 128])
                weights = jnp.exp2(sbuf[now, :, c : c + chunk] * SCALE - peak).astype(BF16)
                part = jnp.dot(weights, v_s[h, row + c : row + c + chunk, :], preferred_element_type=F32)
                total = part if total is None else total + part
            mbuf[later] = most
            q_s[h, row : row + TILE, :] = (total / total[:, HEAD : HEAD + 1]).astype(BF16)

        scores(0, 0)

        def heads(i, carry):
            for j in range(4):
                step(i * 4 + j, j % 2, (j + 1) % 2)
            return carry

        lax.fori_loop(0, HEADS // 4, heads, 0)

    qkvw_copy.wait()
    project(tok[0:256, :], 0, True)
    ring_start(0, 1)
    ring_start(1, 1)
    project(tok[256:512, :], 256, True)
    ring_forward(0, 1)
    ring_forward(1, 1)
    project(tok[512:768, :], 512, True)
    ring_finish(0, 1)
    ring_start(0, 2)

    def inner(i, carry):
        project(halo[1 + i], pl.multiple_of(256 + i * 1024, 256), False)
        return carry

    halo_copies[1].wait_recv()
    halo_copies[2].wait_recv()
    lax.fori_loop(0, 2, inner, 0)
    ring_finish(1, 1)
    attention(1)
    ring_start(1, 2)

    def outer(i, carry):
        project(halo[3 * i], pl.multiple_of(i * 1536, 256), False)
        return carry

    halo_copies[0].wait_recv()
    halo_copies[3].wait_recv()
    lax.fori_loop(0, 2, outer, 0)
    attention(0)
    ring_forward(0, 2)
    attention(2)
    ring_finish(0, 2)
    ring_forward(1, 2)

    outw_copy.wait()
    for h in range(HEADS):
        mixed[:, h * HEAD : (h + 1) * HEAD] = q_s[h, :, 0:HEAD]

    def project_out(i, carry):
        at = pl.ds(pl.multiple_of(i * 256, 256), 256)
        total = tok[at, :].astype(F32) + jnp.dot(mixed[at, :], outw[...], preferred_element_type=F32) + outb[...]
        mixed[at, :] = normalize(total, gains[1:2], shifts[1:2]).astype(BF16)
        acc[at, :] = total + downb[...]
        return carry

    lax.fori_loop(0, 3, project_out, 0)

    def slabs(u, i, slot):
        return pltpu.make_async_copy(
            w.at[i // 2, pl.ds(i % 2 * 2, 2), u, :, :, pl.ds(0, MAIN)], stage.at[slot], stage_sem.at[slot]
        )

    def remainder(u, into):
        copy = pltpu.make_async_copy(w.at[:, :, u, :, :, pl.ds(MAIN, BLOCK - MAIN)], rest, local_sem.at[3])
        copy.start()
        copy.wait()
        for l in range(8):
            piece = rest[:, :, l // 2, l % 2].reshape(256, FFB)
            into[:, l * MAIN : (l + 1) * MAIN] = piece[:, :MAIN]

    def streamed(u, use):
        slabs(u, 0, 0).start()

        def two(i, carry):
            for j in range(2):
                now = 2 * i + j
                slabs(u, now, j).wait()

                @pl.when(now < 7)
                def _():
                    slabs(u, now + 1, 1 - j).start()

                use(now, j)
            return carry

        lax.fori_loop(0, 4, two, 0)

    sibling_finish(0)

    def up(now, slot):
        for j in range(2):
            product = jnp.dot(mixed[...], stage[slot, j].reshape(D, FFB), preferred_element_type=F32)
            hid[2 * now + j] = gelu(product + upb[2 * now + j]).astype(BF16)

    remainder(0, ru)
    streamed(0, up)
    product = lax.dot_general(mixed[...], ru[...], NT, preferred_element_type=F32)
    hid_r[...] = gelu(product + upb_rem[...]).astype(BF16)

    ring_finish(1, 2)
    sibling_finish(1)

    def down(now, slot):
        total = None
        for j in range(2):
            part = lax.dot_general(hid[2 * now + j], stage[slot, j].reshape(D, FFB), NT, preferred_element_type=F32)
            total = part if total is None else total + part
        acc[...] += total

    remainder(1, rd)
    streamed(1, down)
    out[...] = (acc[...] + jnp.dot(hid_r[...], rd[...], preferred_element_type=F32)).astype(BF16)
    for copy in copies:
        copy.wait_send()


def per_device(
    tokens, lengths, norm_gains, norm_shifts, qkv_weight, qkv_bias, out_weight, out_bias, up_weight, up_bias,
    down_weight, down_bias,
):
    wide_pad = ((0, BLOCK - MAIN - REM), (0, FFB - MAIN))
    up_block = jnp.concatenate([up_weight[:, :FFB], jnp.pad(up_weight[:, FFB:].T, wide_pad)], axis=0)
    down_block = jnp.concatenate([down_weight[:FFB].T, jnp.pad(down_weight[FFB:], wide_pad)], axis=0)
    block = jnp.stack([up_block, down_block])
    by_encoder = up_bias.reshape(16, FFB + REM)
    upb = by_encoder[:, None, :FFB]
    upb_rem = jnp.pad(by_encoder[:, FFB:], ((0, 0), (0, 16 - REM))).reshape(1, 256)
    vmem = pl.BlockSpec(memory_space=pltpu.VMEM)
    hbm = pl.BlockSpec(memory_space=pl.ANY)
    dma = pltpu.SemaphoreType.DMA
    out, _ = pl.pallas_call(
        layer_kernel,
        out_shape=[
            jax.ShapeDtypeStruct((ROWS, D), BF16),
            jax.ShapeDtypeStruct((4, 4, 2, 4, 2, BLOCK, FFB), BF16),
        ],
        in_specs=[vmem, vmem, vmem, vmem, hbm, vmem, hbm, vmem, vmem, vmem, vmem, vmem],
        out_specs=[vmem, hbm],
        scratch_shapes=[
            pltpu.VMEM((4, 256, D), BF16),
            pltpu.VMEM((D, 3 * D), BF16),
            pltpu.VMEM((D, D), BF16),
            pltpu.VMEM((HEADS, ROWS, 128), BF16),
            pltpu.VMEM((HEADS, EXT, 128), BF16),
            pltpu.VMEM((HEADS, EXT, 128), BF16),
            pltpu.VMEM((ROWS, 128), BF16),
            pltpu.VMEM((EXT, 128), BF16),
            pltpu.VMEM((256, D), BF16),
            pltpu.VMEM((256, 3 * D), BF16),
            pltpu.VMEM((2, TILE, WINDOW), F32),
            pltpu.VMEM((2, TILE, 128), F32),
            pltpu.VMEM((ROWS, D), BF16),
            pltpu.VMEM((ROWS, D), F32),
            pltpu.VMEM((16, ROWS, FFB), BF16),
            pltpu.VMEM((ROWS, 256), BF16),
            pltpu.VMEM((2, 2, 4, 2, MAIN, FFB), BF16),
            pltpu.VMEM((4, 4, 4, 2, BLOCK - MAIN, FFB), BF16),
            pltpu.VMEM((256, D), BF16),
            pltpu.VMEM((256, D), BF16),
            dma((4,)),
            dma((2,)),
            dma((4,)),
            dma((4,)),
            dma((2, 3, 11)),
            dma((2, 3, 11)),
            dma((2, 3, 5)),
            dma((2, 3, 5)),
        ],
        compiler_params=pltpu.CompilerParams(
            collective_id=0, has_side_effects=True, vmem_limit_bytes=62 * 2**20
        ),
        cost_estimate=pl.CostEstimate(flops=40_000_000_000, bytes_accessed=50_000_000, transcendentals=20_000_000),
    )(
        tokens, lengths, norm_gains, norm_shifts, qkv_weight, qkv_bias[None], out_weight, out_bias[None], block,
        upb, upb_rem, down_bias[None],
    )
    return out


def solution(mesh):
    placed = (
        P(("loader", "encoder"), None),
        P("loader", None),
        P(),
        P(),
        P(),
        P(),
        P(),
        P(),
        P("loader", "encoder"),
        P(),
        P("encoder", "loader"),
        P(),
    )
    return jax.shard_map(
        per_device,
        mesh=mesh,
        in_specs=placed,
        out_specs=P(("loader", "encoder"), None),
        check_vma=False,
    )
```

time: 318 us -> 153 us (0.48)
  the two profiles are of different devices: /device:TPU:6 before, /device:TPU:1 now
where the time goes in v1:
time: 153 us; the launch traced here: 152 us
  Pallas kernels  139 us (91%)
  local copies, waits for them, and re-layouts  12.4 us (8%)
    pallas_call x1, Pallas kernels, per_device(): pl.pallas_call(layer_kernel, out_shape=[jax.ShapeDtypeStruct((ROWS, D), B...  139 us

profile of v1, /device:TPU:1, one launch (start us, length us, event | category | flops | bytes accessed | tf_op | source)
XLA Modules:
  0.0 152.5 jit_solution(5457136023120388374)
XLA Ops:
  0.0 1.3 broadcast_in_dim.13.outb
  1.3 1.3 broadcast_in_dim.15.downb
  2.6 1.3 broadcast_in_dim.12.qkvb
  3.9 0.8 reshape.6
  4.8 0.6 broadcast_in_dim.14.upb
  5.4 0.7 reshape.7.upb_rem
  6.1 0.8 slice.19
  6.8 0.1 copy.15
  6.9 0.8 slice.21
  7.7 0.1 copy.16
  7.8 0.9 slice.18
  8.7 0.9 slice_bitcast_fusion
  9.6 0.7 pad_maximum_fusion.block
  10.3 139.4 %shard_map.118 = (bf16[768,1152]{1,0:T(8,128)(2,1)}, bf16[4,4,2,4,2,160,256]{6,5,4,3,2,1,0:T(8,128)(2,1)}) custom-call(bf16[768,1152]{1,0:T(8,128)(2,1)} %tok.1, s32[1,48]{1,0:T(1,128)} %lens.1, f32[2,1152]{1,0:T(2,128)} %gains.1, f32[2,1152]{1,0:T(2,128)} %shifts.1, bf16[1152,3456]{1,0:T(8,128)(2,1)} %qkvw_hbm.1, f32[1,3456]{1,0:T(1,128)} %broadcast_in_dim.12.qkvb, ...), custom_call_target="tpu_custom_call" | custom-call | flops 40000000000 | bytes 50000000 | tf_op jit(solution)/shard_map/pallas_call | solution.py:371
  149.7 2.8 %copy.18 = bf16[768,1152]{1,0:T(8,128)(2,1)} copy(bf16[768,1152]{1,0:T(8,128)(2,1)} %get-tuple-element.6) | data formatting | bytes 3538944
  (4 shorter events, 0.0 us)

commit v2 on v1

--- a/solution.py
+++ b/solution.py
@@ -17,7 +17,7 @@
 IMAGES = 48
 TILE = 256
 WINDOW = TILE + 2 * REACH
-PARTS = (("xyz", 64, 96), ("yzx", 0, 32), ("xzy", 32, 32))
+PARTS = (("xyz", 96, 64), ("yzx", 0, 48), ("zxy", 48, 48))
 BLOCK = 160
 MAIN = 144
 FFB = 256
@@ -40,9 +40,9 @@
 
 
 def layer_kernel(
-    tok, lens, gains, shifts, qkvw_hbm, qkvb, outw_hbm, outb, block, upb, upb_rem, downb,
+    tok, lens, gains, shifts, qkvw_hbm, qkv_bias, outw_hbm, out_bias, up_own, up_bias, down_own, down_bias,
     out, w,
-    halo, qkvw, outw, q_s, k_s, v_s, qx, kx, first, wide, sbuf, mbuf, mixed, acc, hid, hid_r, stage, rest, ru, rd,
+    block, turned, qkvb, outb, downb, upb, upb_rem, halo, qkvw, outw, q_s, k_s, v_s, qx, kx, first, wide, sbuf, mbuf, mixed, acc, hid, hid_r, stage, rest, ru, rd,
     local_sem, stage_sem, halo_send, halo_recv, send, recv, sib_send, sib_recv,
 ):
     ld, en = lax.axis_index("loader"), lax.axis_index("encoder")
@@ -63,16 +63,27 @@
     qkvw_copy = pltpu.make_async_copy(qkvw_hbm, qkvw, local_sem.at[0])
     outw_copy = pltpu.make_async_copy(outw_hbm, outw, local_sem.at[1])
     own_copy = pltpu.make_async_copy(block, w.at[x, y, :, z, core], local_sem.at[2])
-    own_copy.start()
     qkvw_copy.start()
-    outw_copy.start()
 
     barrier = pltpu.get_barrier_semaphore()
     peers = [device(d, s) for d in "xyz" for s in (1, 2, 3)] + [sibling, right, left]
     for peer in peers:
         pl.semaphore_signal(barrier, inc=1, device_id=peer, device_id_type=MESH)
+
+    block[...] = jnp.zeros_like(block)
+    turned[...] = jnp.zeros_like(turned)
+    block[0, 0:MAIN, :] = up_own[:, 0:FFB]
+    turned[0:MAIN, 0:REM] = up_own[:, FFB : FFB + REM].astype(F32)
+    block[0, MAIN:BLOCK, :] = jnp.transpose(turned[:, 0:128])[0:16].astype(BF16)
+    turned[:, 0:MAIN] = down_own[0:FFB, :].astype(F32)
+    block[1, 0:MAIN, :] = jnp.transpose(turned[...])[0:MAIN].astype(BF16)
+    turned[0:REM, 0:MAIN] = down_own[FFB : FFB + REM, :].astype(F32)
+    turned[REM:16, :] = jnp.zeros((16 - REM, FFB), F32)
+    block[1, MAIN:BLOCK, 0:MAIN] = turned[0:16, 0:MAIN].astype(BF16)
+    own_copy.start()
     pl.semaphore_wait(barrier, len(peers))
     own_copy.wait()
+    outw_copy.start()
 
     copies = []
 
@@ -146,11 +157,26 @@
 
     phase1(0)
     halo_copies = {}
-    for slot, (row, to) in ((1, (512, right)), (2, (0, left)), (0, (256, right)), (3, (256, left))):
+    for slot, (row, to) in ((1, (512, right)), (2, (0, left))):
         halo_copies[slot] = remote(
             tok.at[pl.ds(row, 256)], halo.at[slot], halo_send.at[slot], halo_recv.at[slot], to
         )
     phase1(1)
+    middle = tok.at[pl.ds(256, 256)]
+
+    def outer_copy(slot, to):
+        return pltpu.make_async_remote_copy(
+            src_ref=middle, dst_ref=halo.at[slot], send_sem=halo_send.at[slot], recv_sem=halo_recv.at[slot],
+            device_id=to, device_id_type=MESH,
+        )
+
+    def outer_start():
+        outer_copy(0, right).start()
+        outer_copy(3, left).start()
+
+    def outer_sent():
+        for slot in (0, 3):
+            outer_copy(slot, right).wait_send()
 
     lengths = lens[...]
     sub = lax.broadcasted_iota(jnp.int32, (IMAGES, IMAGES), 0)
@@ -169,6 +195,15 @@
     def lanes(count):
         return lax.broadcasted_iota(jnp.int32, (count, 128), 1)
 
+    qkvb[...] = qkv_bias[...].reshape(1, 3 * D)
+    outb[...] = out_bias[...].reshape(1, D)
+    downb[...] = down_bias[...].reshape(1, D)
+    upb_row = up_bias[...].reshape(1, 16 * (FFB + REM))
+    upb_rem[...] = jnp.zeros_like(upb_rem)
+    for e in range(16):
+        lo = e * (FFB + REM)
+        upb[e] = upb_row[:, lo : lo + FFB]
+        upb_rem[:, e * 16 : e * 16 + REM] = upb_row[:, lo + FFB : lo + FFB + REM]
     for r in range(0, ROWS, 256):
         qx[r : r + 256] = jnp.where(image_lane(256, r), 0.0, 1.0).astype(BF16)
     for r in range(0, EXT, 256):
@@ -252,11 +287,10 @@
     ring_start(0, 1)
     ring_start(1, 1)
     project(tok[256:512, :], 256, True)
+    project(tok[512:768, :], 512, True)
     ring_forward(0, 1)
     ring_forward(1, 1)
-    project(tok[512:768, :], 512, True)
-    ring_finish(0, 1)
-    ring_start(0, 2)
+    outer_start()
 
     def inner(i, carry):
         project(halo[1 + i], pl.multiple_of(256 + i * 1024, 256), False)
@@ -265,22 +299,24 @@
     halo_copies[1].wait_recv()
     halo_copies[2].wait_recv()
     lax.fori_loop(0, 2, inner, 0)
+    ring_finish(0, 1)
+    ring_start(0, 2)
     ring_finish(1, 1)
+    ring_start(1, 2)
     attention(1)
-    ring_start(1, 2)
+    ring_forward(0, 2)
 
     def outer(i, carry):
         project(halo[3 * i], pl.multiple_of(i * 1536, 256), False)
         return carry
 
-    halo_copies[0].wait_recv()
-    halo_copies[3].wait_recv()
+    for slot in (0, 3):
+        outer_copy(slot, right).wait_recv()
     lax.fori_loop(0, 2, outer, 0)
     attention(0)
-    ring_forward(0, 2)
-    attention(2)
     ring_finish(0, 2)
     ring_forward(1, 2)
+    attention(2)
 
     outw_copy.wait()
     for h in range(HEADS):
@@ -294,6 +330,7 @@
         return carry
 
     lax.fori_loop(0, 3, project_out, 0)
+    ring_finish(1, 2)
 
     def slabs(u, i, slot):
         return pltpu.make_async_copy(
@@ -337,7 +374,6 @@
     product = lax.dot_general(mixed[...], ru[...], NT, preferred_element_type=F32)
     hid_r[...] = gelu(product + upb_rem[...]).astype(BF16)
 
-    ring_finish(1, 2)
     sibling_finish(1)
 
     def down(now, slot):
@@ -350,6 +386,7 @@
     remainder(1, rd)
     streamed(1, down)
     out[...] = (acc[...] + jnp.dot(hid_r[...], rd[...], preferred_element_type=F32)).astype(BF16)
+    outer_sent()
     for copy in copies:
         copy.wait_send()
 
@@ -358,13 +395,6 @@
     tokens, lengths, norm_gains, norm_shifts, qkv_weight, qkv_bias, out_weight, out_bias, up_weight, up_bias,
     down_weight, down_bias,
 ):
-    wide_pad = ((0, BLOCK - MAIN - REM), (0, FFB - MAIN))
-    up_block = jnp.concatenate([up_weight[:, :FFB], jnp.pad(up_weight[:, FFB:].T, wide_pad)], axis=0)
-    down_block = jnp.concatenate([down_weight[:FFB].T, jnp.pad(down_weight[FFB:], wide_pad)], axis=0)
-    block = jnp.stack([up_block, down_block])
-    by_encoder = up_bias.reshape(16, FFB + REM)
-    upb = by_encoder[:, None, :FFB]
-    upb_rem = jnp.pad(by_encoder[:, FFB:], ((0, 0), (0, 16 - REM))).reshape(1, 256)
     vmem = pl.BlockSpec(memory_space=pltpu.VMEM)
     hbm = pl.BlockSpec(memory_space=pl.ANY)
     dma = pltpu.SemaphoreType.DMA
@@ -377,6 +407,13 @@
         in_specs=[vmem, vmem, vmem, vmem, hbm, vmem, hbm, vmem, vmem, vmem, vmem, vmem],
         out_specs=[vmem, hbm],
         scratch_shapes=[
+            pltpu.VMEM((2, BLOCK, FFB), BF16),
+            pltpu.VMEM((FFB, FFB), F32),
+            pltpu.VMEM((1, 3 * D), F32),
+            pltpu.VMEM((1, D), F32),
+            pltpu.VMEM((1, D), F32),
+            pltpu.VMEM((16, 1, FFB), F32),
+            pltpu.VMEM((1, 256), F32),
             pltpu.VMEM((4, 256, D), BF16),
             pltpu.VMEM((D, 3 * D), BF16),
             pltpu.VMEM((D, D), BF16),
@@ -411,8 +448,8 @@
         ),
         cost_estimate=pl.CostEstimate(flops=40_000_000_000, bytes_accessed=50_000_000, transcendentals=20_000_000),
     )(
-        tokens, lengths, norm_gains, norm_shifts, qkv_weight, qkv_bias[None], out_weight, out_bias[None], block,
-        upb, upb_rem, down_bias[None],
+        tokens, lengths, norm_gains, norm_shifts, qkv_weight, qkv_bias, out_weight, out_bias, up_weight, up_bias,
+        down_weight, down_bias,
     )
     return out
 

time: 153 us -> 132 us (0.86)
  the two profiles are of different devices: /device:TPU:1 before, /device:TPU:4 now
where the time goes in v2:
time: 132 us
  Pallas kernels  127 us (96%)
  local copies, waits for them, and re-layouts  4.48 us (3%)
    pallas_call x1, Pallas kernels, per_device(): pl.pallas_call(layer_kernel, out_shape=[jax.ShapeDtypeStruct((ROWS, D), B...  127 us
    unnamed x2, local copies, waits for them, and re-layouts  4.48 us

profile of v2, /device:TPU:4, one launch (start us, length us, event | category | flops | bytes accessed | tf_op | source)
XLA Modules:
  0.0 131.5 jit_solution(3645685229797010964)
XLA Ops:
  0.0 1.7 %copy.13.down_own = bf16[269,144]{1,0:T(8,128)(2,1)} copy(bf16[269,144]{0,1:T(8,128)(2,1)} %param.22) | data formatting | bytes 154944 | tf_op args[10]
  1.7 127.0 %shard_map.118 = (bf16[768,1152]{1,0:T(8,128)(2,1)}, bf16[4,4,2,4,2,160,256]{6,5,4,3,2,1,0:T(8,128)(2,1)}) custom-call(bf16[768,1152]{1,0:T(8,128)(2,1)} %tok.1, s32[1,48]{1,0:T(1,128)} %lens.1, f32[2,1152]{1,0:T(2,128)} %gains.1, f32[2,1152]{1,0:T(2,128)} %shifts.1, bf16[1152,3456]{1,0:T(8,128)(2,1)} %qkvw_hbm.1, f32[3456]{0:T(1024)} %qkv_bias.1, ...), custom_call_target="tpu_custom_call" | custom-call | flops 40000000000 | bytes 50000000 | tf_op jit(solution)/shard_map/pallas_call | solution.py:401
  128.7 2.8 %copy.15 = bf16[768,1152]{1,0:T(8,128)(2,1)} copy(bf16[768,1152]{1,0:T(8,128)(2,1)} %get-tuple-element.6) | data formatting | bytes 3538944

commit v3 on v2

--- a/solution.py
+++ b/solution.py
@@ -156,12 +156,12 @@
                 pending[u, i, "s", slot].wait_recv()
 
     phase1(0)
+    phase1(1)
     halo_copies = {}
     for slot, (row, to) in ((1, (512, right)), (2, (0, left))):
         halo_copies[slot] = remote(
             tok.at[pl.ds(row, 256)], halo.at[slot], halo_send.at[slot], halo_recv.at[slot], to
         )
-    phase1(1)
     middle = tok.at[pl.ds(256, 256)]
 
     def outer_copy(slot, to):
@@ -304,7 +304,6 @@
     ring_finish(1, 1)
     ring_start(1, 2)
     attention(1)
-    ring_forward(0, 2)
 
     def outer(i, carry):
         project(halo[3 * i], pl.multiple_of(i * 1536, 256), False)
@@ -313,6 +312,7 @@
     for slot in (0, 3):
         outer_copy(slot, right).wait_recv()
     lax.fori_loop(0, 2, outer, 0)
+    ring_forward(0, 2)
     attention(0)
     ring_finish(0, 2)
     ring_forward(1, 2)

time: 132 us -> 130 us (0.985)
  the two profiles are of different devices: /device:TPU:4 before, /device:TPU:6 now
where the time goes in v3:
time: 130 us; the launch traced here: 127 us
  Pallas kernels  123 us (95%)
  local copies, waits for them, and re-layouts  4.48 us (3%)
    pallas_call x1, Pallas kernels, per_device(): pl.pallas_call(layer_kernel, out_shape=[jax.ShapeDtypeStruct((ROWS, D), B...  123 us
    unnamed x2, local copies, waits for them, and re-layouts  4.48 us

profile of v3, /device:TPU:6, one launch (start us, length us, event | category | flops | bytes accessed | tf_op | source)
XLA Modules:
  0.0 127.2 jit_solution(16613155140735849540)
XLA Ops:
  0.0 1.7 %copy.13.down_own = bf16[269,144]{1,0:T(8,128)(2,1)} copy(bf16[269,144]{0,1:T(8,128)(2,1)} %param.22) | data formatting | bytes 154944 | tf_op args[10]
  1.7 122.8 %shard_map.118 = (bf16[768,1152]{1,0:T(8,128)(2,1)}, bf16[4,4,2,4,2,160,256]{6,5,4,3,2,1,0:T(8,128)(2,1)}) custom-call(bf16[768,1152]{1,0:T(8,128)(2,1)} %tok.1, s32[1,48]{1,0:T(1,128)} %lens.1, f32[2,1152]{1,0:T(2,128)} %gains.1, f32[2,1152]{1,0:T(2,128)} %shifts.1, bf16[1152,3456]{1,0:T(8,128)(2,1)} %qkvw_hbm.1, f32[3456]{0:T(1024)} %qkv_bias.1, ...), custom_call_target="tpu_custom_call" | custom-call | flops 40000000000 | bytes 50000000 | tf_op jit(solution)/shard_map/pallas_call | solution.py:401
  124.4 2.8 %copy.15 = bf16[768,1152]{1,0:T(8,128)(2,1)} copy(bf16[768,1152]{1,0:T(8,128)(2,1)} %get-tuple-element.6) | data formatting | bytes 3538944
